TPU v7x, 128 devices: a whole 4x4x4 slice. The times are simulated.
128 devices in a mesh: feat: 8 (over x, z_hi), hid: 16 (over z_lo, y, core).
Axes of the slice: x: 4, y: 4, z: 4 (z_hi: 2, z_lo: 2; z = z_hi * 2 + z_lo), core: 2. Of those that a mesh axis runs over, the one named last changes fastest.
Arguments:
- tokens: bfloat16 [4096, 12288], P('feat'), may hold values from -6 to 6
- preact: bfloat16 [4096, 24576], P('feat', 'hid'), may hold values from -6 to 6
- grad_hidden: bfloat16 [4096, 24576], P('feat', 'hid'), may hold values from -0.59765625 to 0.59765625
- w_packed: bfloat16 [12288, 8192], P('feat', 'hid'), may hold values from -0.109375 to 0.109375
- block_cols: int32 [96, 64], P('feat', 'hid'), may hold values from 0 to 11, as said below
- block_counts: int32 [96, 16], P('feat', 'hid'), may hold values from 2 to 4, as said below
Outputs:
- grad_input: bfloat16 [4096, 12288], P('feat', 'hid')
- grad_weight: bfloat16 [12288, 8192], P('feat', 'hid')
Inputs may be any that keep to these rules, and one draw needn't show every extreme that they name: `block_cols`: within one block row and hidden group, the 4 slots hold distinct block columns; slots at or after the count are dead. `block_counts`: in every hidden group some block row has all 4 slots live.
All inputs are finite; a program needn't handle non-finite values.
Results may differ from a plain program's by a relative error of at most 0.022.
Values may be sent and summed in bfloat16 or wider, within the bound.
A program may use at most 256 MiB of HBM per device.

v0:
```python
import jax
import jax.numpy as jnp
from jax import lax
from jax.sharding import PartitionSpec as P

BLOCK = 128


CUBIC = 0.044715
ROOT = 0.7978845608028654


def gelu_slope(values):
    tangent = jnp.tanh(ROOT * (values + CUBIC * values * values * values))
    return 0.5 * (1.0 + tangent) + 0.5 * values * (1.0 - tangent * tangent) * ROOT * (
        1.0 + 3.0 * CUBIC * values * values
    )


def pick_blocks(grad_panel, col_ids):
    panel_rows = grad_panel.shape[0]
    local_cols = grad_panel.shape[1] // BLOCK
    grad_three = grad_panel.reshape(panel_rows, local_cols, BLOCK)
    selector = (
        col_ids[:, :, None] == jnp.arange(local_cols, dtype=jnp.int32)[None, None, :]
    ).astype(jnp.bfloat16)
    chosen = jnp.einsum("tcj,bsc->tbsj", grad_three, selector, preferred_element_type=jnp.float32)
    return chosen.astype(jnp.bfloat16)


def live_slots(counts, slot_count):
    return jnp.arange(slot_count, dtype=jnp.int32)[None, :] < counts


def per_device(tokens, preact, grad_hidden, w_packed, block_cols, block_counts):
    panel_rows = tokens.shape[0]
    slot_count = block_cols.shape[1]
    rows_dev = w_packed.shape[0] // BLOCK
    grad_pre = (grad_hidden.astype(jnp.float32) * gelu_slope(preact.astype(jnp.float32))).astype(
        jnp.bfloat16
    )
    pattern_cols, pattern_counts = (
        lax.all_gather(block_cols, "feat", axis=0, tiled=True),
        lax.all_gather(block_counts, "feat", axis=0, tiled=True),
    )

    def one_group(group_index):
        row_start = group_index * rows_dev
        col_ids = lax.dynamic_slice_in_dim(pattern_cols, row_start, rows_dev, 0)
        counts = lax.dynamic_slice_in_dim(pattern_counts, row_start, rows_dev, 0)
        chosen = pick_blocks(grad_pre, col_ids)
        features = lax.dynamic_slice_in_dim(tokens, row_start * BLOCK, rows_dev * BLOCK, 1)
        features = features.reshape(panel_rows, rows_dev, BLOCK)
        weight_term = jnp.einsum(
            "tbi,tbsj->bisj", features, chosen, preferred_element_type=jnp.float32
        )
        weight_term = weight_term * live_slots(counts, slot_count)[:, None, :, None].astype(
            jnp.float32
        )
        return weight_term.reshape(rows_dev * BLOCK, slot_count * BLOCK)

    group_terms = lax.map(
        one_group,
        jnp.arange(rows_dev * BLOCK * lax.axis_size("feat") // (rows_dev * BLOCK), dtype=jnp.int32),
    )
    summed = lax.psum_scatter(
        group_terms.reshape(rows_dev * BLOCK * lax.axis_size("feat"), slot_count * BLOCK).astype(
            jnp.bfloat16
        ),
        "feat",
        scatter_dimension=0,
        tiled=True,
    )
    weight_slab = lax.all_gather(w_packed, "feat", axis=0, tiled=True)
    block_rows = weight_slab.shape[0] // BLOCK
    row_start = jnp.int32(0) // BLOCK
    col_ids = pattern_cols
    counts = pattern_counts
    chosen = pick_blocks(grad_pre, col_ids)
    slab_mask = live_slots(counts, slot_count)[:, None, :, None].astype(jnp.bfloat16)
    weights = weight_slab.reshape(block_rows, BLOCK, slot_count, BLOCK) * slab_mask
    result = jnp.einsum("tbsj,bisj->tbi", chosen, weights, preferred_element_type=jnp.float32)
    partial_input = result.reshape(panel_rows, block_rows * BLOCK)
    grad_input = lax.psum_scatter(
        partial_input.astype(jnp.bfloat16), "hid", scatter_dimension=1, tiled=True
    )
    return (grad_input, summed)


def solution(mesh):
    placed = (
        P("feat", None),
        P("feat", "hid"),
        P("feat", "hid"),
        P("feat", "hid"),
        P("feat", "hid"),
        P("feat", "hid"),
    )
    return jax.shard_map(
        per_device,
        mesh=mesh,
        in_specs=placed,
        out_specs=(P("feat", "hid"), P("feat", "hid")),
        check_vma=False,
    )
```

profile of v0, /device:TPU:2, one launch (start us, length us, event | category | flops | bytes accessed | tf_op | source)
XLA Modules:
  0.0 448.5 jit_solution(13879283648291082071)
XLA Ops:
  8.0 29.8 %all-gather = s32[8,12,4]{1,2,0:T(4,128)S(1)} all-gather(s32[1,12,4]{1,2,0:T(4,128)} %bitcast.69), channel_id=1, replica_groups=mesh['feat'=8,'hid'=16] {'feat'}, dimensions={0}, use_global_device_ids=true | all-gather | bytes 1728 | tf_op jit(solution)/shard_map/all_gather | solution.py:43
  42.4 11.3 %all-reduce = s32[96]{0:T(128)S(1)} all-reduce(s32[96]{0:T(128)S(1)} %bitcast_dynamic-update-slice_fusion), channel_id=1, replica_groups=mesh['feat'=8,'hid'=16] {'feat'}, use_global_device_ids=true, to_apply=%add | all-reduce | flops 96 | bytes 768
  53.7 3.3 fusion.23
  57.1 147.3 %while.12 = (s32[]{:T(128)}, bf16[8,1536,512]{2,1,0:T(8,128)(2,1)}, s32[8]{0:T(128)S(1)}, bf16[512,12288]{1,0:T(8,128)(2,1)}, s32[96,4]{0,1:T(4,128)S(1)}, /*ind...) while((s32[]{:T(128)}, bf16[8,1536,512]{2,1,0:T(8,128)(2,1)}, ...), condition=%wide.region_2.3_spmd, body=%wide.region_1.2_spmd.sunk | while | flops 885523136 | bytes 55051680 | solution.py:62
  62.4 3.4 copy.56
  68.2 3.5 fusion.44
  80.9 3.3 copy.56
  86.6 3.5 fusion.44
  99.3 3.3 copy.56
  102.6 2.4 convert_bitcast_fusion.3
  105.0 3.5 fusion.44
  117.7 3.3 copy.56
  121.0 2.4 convert_bitcast_fusion.3
  123.4 3.5 fusion.44
  136.0 3.4 copy.56
  141.8 3.5 fusion.44
  154.5 3.3 copy.56
  157.8 2.4 convert_bitcast_fusion.3
  160.2 3.5 fusion.44
  172.9 3.3 copy.56
  176.2 2.4 convert_bitcast_fusion.3
  178.6 3.5 fusion.44
  191.2 3.3 copy.56
  194.6 2.4 convert_bitcast_fusion.3
  197.0 3.5 fusion.44
  204.6 3.0 copy.29
  207.7 22.2 %convert_bitcast_fusion.1 = bf16[512,96,4,128]{3,1,0,2:T(8,128)(2,1)} fusion(bf16[512,12,128]{2,1,0:T(8,128)(2,1)} %copy.29, s32[96,4]{0,1:T(4,128)S(1)} %get-tuple-element.220), kind=kOutput, calls=%fused_computation.17 | convolution fusion | flops 629150208 | bytes 51906048 | tf_op jit(solution)/shard_map/tcj,bsc->tbsj/dot_general | solution.py:27
  229.9 18.3 %reshape.83 = bf16[96,128,4,128]{3,2,1,0:T(4,128)(2,1)} reshape(bf16[12288,512]{1,0:T(8,128)(2,1)} %all-gather.3.cloned.1.call-done) | data formatting | bytes 25165824 | tf_op jit(solution)/shard_map/reshape | solution.py:81
  248.2 41.8 %bitcast_convert_fusion = bf16[96,128,512]{2,1,0:T(8,128)(2,1)} fusion(bf16[512,96,4,128]{3,1,0,2:T(8,128)(2,1)} %convert_bitcast_fusion.1, bf16[96,128,4,128]{3,2,1,0:T(4,128)(2,1)} %reshape.83, bf16[96,4]{1,0:T(8,128)(2,1)S(1)} %fusion.26), kind=kOutput, calls=%fused_computation.18 | convolution fusion | flops 6455033856 | bytes 75498240 | tf_op jit(solution)/shard_map/tbsj,bisj->tbi/dot_general | solution.py:82
  290.0 16.8 %copy.31 = bf16[512,12288]{1,0:T(8,128)(2,1)} copy(bf16[512,12288]{0,1:T(8,128)(2,1)} %bitcast.68) | data formatting | bytes 25165824 | tf_op jit(solution)/shard_map/convert_element_type | solution.py:85
  306.8 50.3 %reduce-scatter.5.cloned.1.call-done = bf16[1536,512]{1,0:T(8,128)(2,1)} async-done(((bf16[12288,512]{1,0:T(8,128)(2,1)}), bf16[1536,512]{1,0:T(8,128)(2,1)}) %reduce-scatter.5.cloned.1.call-update) | async-done | bytes 1572880 | tf_op jit(solution)/shard_map/reduce_scatter | solution.py:66
  357.1 84.9 %reduce-scatter.3.cloned.1.call-done = bf16[512,768]{1,0:T(8,128)(2,1)} async-done(((bf16[512,12288]{1,0:T(8,128)(2,1)}), bf16[512,768]{1,0:T(8,128)(2,1)}) %reduce-scatter.3.cloned.1.call-update) | async-done | bytes 786448 | tf_op jit(solution)/shard_map/reduce_scatter | solution.py:84
  (146 shorter events, 74.9 us)
Async XLA Ops:
  7.2 32.4 %copy-start.3 = (bf16[512,1536]{1,0:T(8,128)(2,1)S(1)}, bf16[512,1536]{1,0:T(8,128)(2,1)}, u32[]{:S(2)}) copy-start(bf16[512,1536]{1,0:T(8,128)(2,1)} %param.10) | copy-start | bytes 4718596
  7.2 222.7 %all-gather.3.cloned.1.call-start = ((), (), s32[]{:S(2)}) async-start(), calls=%async_computation.2 | async-start | bytes 14155776 | tf_op jit(solution)/shard_map/all_gather | solution.py:74
  7.9 349.2 %reduce-scatter.5.cloned.1.call-start = ((), (), s32[]{:S(2)}) async-start(), calls=%async_computation.4 | async-start | bytes 14155776 | tf_op jit(solution)/shard_map/reduce_scatter | solution.py:66
  37.8 3.4 copy-start.5
  37.8 4.5 %copy-start.4 = (s32[12,1]{0,1:T(1,128)S(1)}, s32[12,1]{0,1:T(1,128)}, u32[]{:S(2)}) copy-start(s32[12,1]{0,1:T(1,128)} %param.13) | copy-start | bytes 148
  57.1 2.1 copy-start
  65.8 2.4 copy-start.2
  73.6 2.0 copy-start.1
  75.6 2.1 copy-start
  84.2 2.4 copy-start.2
  92.0 2.0 copy-start.1
  94.0 2.1 copy-start
  102.6 2.4 copy-start.2
  110.4 2.0 copy-start.1
  112.4 2.1 copy-start
  121.0 2.4 copy-start.2
  128.8 2.0 copy-start.1
  130.8 2.1 copy-start
  139.4 2.4 copy-start.2
  147.2 2.0 copy-start.1
  149.2 2.1 copy-start
  157.8 2.4 copy-start.2
  165.6 2.0 copy-start.1
  167.6 2.1 copy-start
  176.2 2.4 copy-start.2
  184.0 2.0 copy-start.1
  185.9 2.1 copy-start
  194.6 2.4 copy-start.2
  202.4 2.0 copy-start.1
  204.4 237.6 %reduce-scatter.3.cloned.1.call-start = ((), (), s32[]{:S(2)}) async-start(), calls=%async_computation.3 | async-start | bytes 13369344 | tf_op jit(solution)/shard_map/reduce_scatter | solution.py:84
Sparse Core Ops, SparseCore 0:
  10.3 148.8 all-gather.2
  204.5 152.5 reduce-scatter.4
  360.2 81.7 reduce-scatter.2
where the time goes:
time: 451 us; the launch traced here: 449 us
  waiting for transfers between devices  136 us (30%)
  local copies, waits for them, and re-layouts  131 us (29%)
  matrix products  111 us (25%)
  blocking collectives  41 us (9%)
  between operations  14.4 us (3%)
  loops' own time  11 us (2%)
    reduce_scatter x1, waiting for transfers between devices, per_device(): lax.psum_scatter(partial_input.astype(jnp.bfloat16), 'hid', scatter_dimen...  84.9 us
    reduce_scatter x1, waiting for transfers between devices, per_device(): lax.psum_scatter(group_terms.reshape(rows_dev * BLOCK * lax.axis_size('fe...  50.3 us
    dot_general x1, matrix products, per_device(): jnp.einsum('tbsj,bisj->tbi', chosen, weights, preferred_element_type=jnp....  41.8 us
    dot_general x9, matrix products, pick_blocks(): jnp.einsum('tcj,bsc->tbsj', grad_three, selector, preferred_element_type=...  41.1 us
    reshape x9, local copies, waits for them, and re-layouts, pick_blocks(): grad_three = grad_panel.reshape(panel_rows, local_cols, BLOCK)  29.8 us
    all_gather x1, blocking collectives, per_device(): lax.all_gather(block_cols, 'feat', axis=0, tiled=True)  29.8 us
    dot_general x8, matrix products, one_group(): jnp.einsum('tbi,tbsj->bisj', features, chosen, preferred_element_type=jnp...  27.9 us
    dynamic_slice x16, local copies, waits for them, and re-layouts, one_group(): lax.dynamic_slice_in_dim(tokens, row_start * BLOCK, rows_dev * BLOCK, 1)  24.7 us
  transfers between devices with their start and end apart: 3, of which 2 were waited for; matrix products, arithmetic and copies ran while one was open for 54% of the time, Pallas kernels for 0%

commit v1 on v0

v1 whole, which is shorter than its diff:
```python
import functools

import jax
import jax.numpy as jnp
from jax import lax
from jax.experimental import pallas as pl
from jax.experimental.pallas import tpu as pltpu
from jax.sharding import PartitionSpec as P

BLOCK = 128
SLOTS = 4
PANEL = 512
ROWS_DEV = 12
WIDE = ROWS_DEV * BLOCK
HALF = WIDE // 2
COLS = 12
CUBIC = 0.044715
ROOT = 0.7978845608028654
MESH = pl.DeviceIdType.MESH
OWN, RIGHT, LEFT, FAR = 0, 1, 2, 3
X_STEP = (0, 1, 3, 2)
UNITS = (
    (0, OWN), (0, RIGHT), (0, LEFT), (1, OWN), (1, RIGHT), (1, LEFT), (0, FAR), (1, FAR),
)


def gelu_slope(values):
    tangent = jnp.tanh(ROOT * (values + CUBIC * values * values * values))
    return 0.5 * (1.0 + tangent) + 0.5 * values * (1.0 - tangent * tangent) * ROOT * (
        1.0 + 3.0 * CUBIC * values * values
    )


def add_rows(dst, dst_row, dst_cols, terms, rows, step=16):
    def body(i, carry):
        off = i * step
        here = (pl.ds(pl.multiple_of(dst_row + off, 16), step), dst_cols)
        total = dst[here].astype(jnp.float32)
        for ref, row, cols in terms:
            total = total + ref[pl.ds(pl.multiple_of(row + off, 16), step), cols].astype(jnp.float32)
        dst[here] = total.astype(jnp.bfloat16)
        return carry

    lax.fori_loop(0, rows // step, body, 0)


def kernel(
    pat_ref, tokens, preact, grad_hidden, w_hbm,
    gi_ref, gw_ref, tp_ref,
    pat_in, pat_s, w_all, g_own, g_peer, tok_s, part, rb1, r2, rb3, dw, dx,
    send, recv, local,
):
    f, h = lax.axis_index("feat"), lax.axis_index("hid")
    x, zh, zl, y, c = f // 2, f % 2, h // 8, (h // 2) % 4, h % 2

    def dev(x_, zh_, zl_, y_, c_):
        return (x_ * 2 + zh_, zl_ * 8 + y_ * 2 + c_)

    xg = [(x + s) % 4 for s in X_STEP]
    core = dev(x, zh, zl, y, 1 - c)
    xr, xl, xo = dev(xg[RIGHT], zh, zl, y, c), dev(xg[LEFT], zh, zl, y, c), dev(xg[FAR], zh, zl, y, c)
    yr, yl = dev(x, zh, zl, (y + 1) % 4, c), dev(x, zh, zl, (y + 3) % 4, c)
    zlp, zhp = dev(x, zh, 1 - zl, y, c), dev(x, 1 - zh, zl, y, c)

    count = {"remote": 0, "local": 1}
    sends = []

    def remote(src, dst, device):
        i = count["remote"]
        count["remote"] += 1
        cp = pltpu.make_async_remote_copy(
            src_ref=src, dst_ref=dst, send_sem=send.at[i], recv_sem=recv.at[i],
            device_id=device, device_id_type=MESH,
        )
        sends.append(cp)
        return cp

    def near(src, dst):
        i = count["local"]
        count["local"] += 1
        return pltpu.make_async_copy(src, dst, local.at[i])

    pre_in, gh_in = near(preact, part.at[6]), near(grad_hidden, part.at[7])
    w_in = near(w_hbm, w_all.at[OWN])
    pat_own = near(pat_ref, pat_s.at[OWN])
    for cp in (pre_in, gh_in, w_in, pat_own):
        cp.start()

    barrier = pltpu.get_barrier_semaphore()

    def greet(device):
        pl.semaphore_signal(barrier, inc=1, device_id=device, device_id_type=MESH)

    for device in (core, xr, xl, xo, yr, yl, zlp, zhp):
        greet(device)
    mine = (y % 2) == zh
    for other in range(16):
        skip = jnp.logical_and(mine, h == other)

        @pl.when(jnp.logical_not(skip))
        def _():
            greet((x * 2 + y % 2, jnp.int32(other)))

    pl.semaphore_wait(barrier, 24 - mine.astype(jnp.int32))

    pats = [
        remote(pat_ref, pat_in.at[0], xr), remote(pat_ref, pat_in.at[1], xl), remote(pat_ref, pat_in.at[2], xo),
    ]
    w_right = remote(w_hbm, w_all.at[LEFT], xr)
    w_left = remote(w_hbm, w_all.at[RIGHT], xl)
    for cp in pats:
        cp.start()
    w_right.start()
    w_left.start()

    piece = pl.multiple_of(c * 256 + y * 64, 64)
    rows_of = lambda at, n: pl.ds(pl.multiple_of(at, 16), n)

    def group_cols(k, zh_):
        return pl.ds(pl.multiple_of((2 * xg[k] + zh_) * WIDE, 128), WIDE)

    t0 = {
        k: remote(tokens.at[pl.ds(piece, 64), group_cols(k, 1 - zh)], tp_ref.at[k, pl.ds(piece, 64)], zhp)
        for k in range(4)
    }
    t0[FAR].start()
    t0[RIGHT].start()

    pre_in.wait()
    gh_in.wait()

    def slope_step(i, carry):
        rows = pl.ds(pl.multiple_of(i * 16, 16), 16)
        value = part[6, rows, :].astype(jnp.float32)
        grad = (part[7, rows, :].astype(jnp.float32) * gelu_slope(value)).astype(jnp.bfloat16)
        for b in range(COLS):
            g_own[b, rows, :] = grad[:, b * BLOCK:(b + 1) * BLOCK]
        return carry

    lax.fori_loop(0, PANEL // 16, slope_step, 0)
    g_send = remote(g_own, g_peer, zhp)
    g_send.start()
    w_in.wait()
    pat_own.wait()

    def selected(panel, k, r):
        grad = (g_own, g_peer)[panel]
        return jnp.concatenate([grad[pat_s[k, r, s]] for s in range(SLOTS)], axis=1)

    lanes = lambda: lax.broadcasted_iota(jnp.int32, (BLOCK, SLOTS * BLOCK), 1)

    def partial_unit(u):
        panel, k = UNITS[u]

        def body(i, carry):
            for v in range(2):
                r = 2 * i + v
                at = pl.ds(pl.multiple_of(r * BLOCK, BLOCK), BLOCK)
                weights = jnp.where(
                    lanes() < pat_s[k, r, SLOTS] * BLOCK, w_all[k, at, :], jnp.zeros((), jnp.bfloat16)
                )
                part[u, :, at] = lax.dot_general(
                    selected(panel, k, r), weights, (((1,), (1,)), ((), ())),
                    preferred_element_type=jnp.float32,
                ).astype(jnp.bfloat16)
            return carry

        lax.fori_loop(0, ROWS_DEV // 2, body, 0)

    def weight_unit(k, slot):
        def body(r, carry):
            at = pl.ds(pl.multiple_of(r * BLOCK, BLOCK), BLOCK)
            total = 0.0
            for panel in range(2):
                total = total + lax.dot_general(
                    tok_s[slot, panel, :, at], selected(panel, k, r), (((0,), (0,)), ((), ())),
                    preferred_element_type=jnp.float32,
                )
            total = jnp.where(lanes() < pat_s[k, r, SLOTS] * BLOCK, total, 0.0)
            dw[k, at, :] = total.astype(jnp.bfloat16)
            return carry

        lax.fori_loop(0, ROWS_DEV, body, 0)

    A, B = pl.ds(0, HALF), pl.ds(HALF, HALF)
    chunk = lambda t: pl.multiple_of(c * 256 + ((y + t) % 4) * 64, 64)
    stage = {}

    def start_core(u):
        cp = remote(part.at[u, rows_of((1 - c) * 256, 256)], rb1.at[u], core)
        cp.start()
        stage[u, 1] = cp

    def start_ring(u):
        stage[u, 1].wait_recv()
        add_rows(part.at[u], c * 256, slice(None), [(rb1.at[u], 0, slice(None))], 256)
        cps = [
            remote(part.at[u, rows_of(chunk(2), 64), A], r2.at[u, 0], yr),
            remote(part.at[u, rows_of(chunk(2), 64), B], r2.at[u, 1], yl),
            remote(part.at[u, rows_of(chunk(1), 64), B], r2.at[u, 2], yr),
            remote(part.at[u, rows_of(chunk(3), 64), A], r2.at[u, 3], yl),
        ]
        for cp in cps:
            cp.start()
        stage[u, 2] = cps

    def step_ring(u):
        cps = stage[u, 2]
        cps[0].wait_recv()
        add_rows(part.at[u], chunk(1), A, [(r2.at[u, 0], 0, slice(None))], 64)
        right = remote(part.at[u, rows_of(chunk(1), 64), A], r2.at[u, 4], yr)
        right.start()
        cps[1].wait_recv()
        add_rows(part.at[u], chunk(3), B, [(r2.at[u, 1], 0, slice(None))], 64)
        left = remote(part.at[u, rows_of(chunk(3), 64), B], r2.at[u, 5], yl)
        left.start()
        stage[u, 3] = (right, left)

    def end_ring(u):
        stage[u, 2][3].wait_recv()
        stage[u, 3][0].wait_recv()
        every = slice(None)
        add_rows(part.at[u], chunk(0), A, [(r2.at[u, 3], 0, every), (r2.at[u, 4], 0, every)], 64)
        stage[u, 2][2].wait_recv()
        stage[u, 3][1].wait_recv()
        add_rows(part.at[u], chunk(0), B, [(r2.at[u, 2], 0, every), (r2.at[u, 5], 0, every)], 64)
        cp = remote(part.at[u, rows_of(chunk(0) + (1 - zl) * 32, 32)], rb3.at[u], zlp)
        cp.start()
        stage[u, 4] = cp

    finals = []

    def to_owner(u):
        panel, k = UNITS[u]
        stage[u, 4].wait_recv()
        keep = chunk(0) + zl * 32
        add_rows(part.at[u], keep, slice(None), [(rb3.at[u], 0, slice(None))], 32)
        for j, cols in enumerate((A, B)):
            owner_h = 4 * xg[k] + 2 * zh + j
            owner_f = x * 2 + (zh if panel == 0 else 1 - zh)
            src = part.at[u, rows_of(keep, 32), cols]
            dst = gi_ref.at[rows_of(keep, 32)]
            i = count["remote"]
            count["remote"] += 1
            cp = pltpu.make_async_remote_copy(
                src_ref=src, dst_ref=dst, send_sem=send.at[i], recv_sem=local.at[0],
                device_id=(owner_f, owner_h), device_id_type=MESH,
            )
            if panel == 0:
                here = owner_h == h
                stay = pltpu.make_async_copy(src, dst, local.at[0])

                @pl.when(here)
                def _():
                    stay.start()

                @pl.when(jnp.logical_not(here))
                def _():
                    cp.start()
            else:
                here = None
                cp.start()
            finals.append((cp, here))

    t1, t2, t3 = {}, {}, {}

    def tok_spread(k):
        t0[k].wait_recv()
        at = tp_ref.at[k, pl.ds(piece, 64)]
        t1[k] = (remote(at, at, yr), remote(at, at, yl))
        for cp in t1[k]:
            cp.start()

    def tok_forward(k):
        t1[k][0].wait_recv()
        at = tp_ref.at[k, rows_of(chunk(3), 32)]
        right = remote(at, at, yr)
        right.start()
        t1[k][1].wait_recv()
        at = tp_ref.at[k, rows_of(chunk(1) + 32, 32)]
        left = remote(at, at, yl)
        left.start()
        t2[k] = (right, left)

    def tok_core(k):
        for cp in t2[k]:
            cp.wait_recv()
        at = tp_ref.at[k, rows_of(c * 256, 256)]
        t3[k] = remote(at, at, core)
        t3[k].start()

    loads = {}

    def load_own(k, slot):
        loads[k, 0] = near(tokens.at[:, group_cols(k, zh)], tok_s.at[slot, 0])
        loads[k, 0].start()

    def load_peer(k, slot):
        t3[k].wait_recv()
        loads[k, 1] = near(tp_ref.at[k], tok_s.at[slot, 1])
        loads[k, 1].start()

    def weight_group(k, slot):
        loads[k, 0].wait()
        loads[k, 1].wait()
        weight_unit(k, slot)

    partial_unit(0)
    start_core(0)
    load_own(FAR, 0)
    load_own(RIGHT, 1)
    start_ring(0)
    tok_spread(FAR)
    tok_spread(RIGHT)
    step_ring(0)
    tok_forward(FAR)
    end_ring(0)
    tok_forward(RIGHT)
    to_owner(0)
    t0[LEFT].start()
    t0[OWN].start()
    tok_core(FAR)
    tok_core(RIGHT)
    load_peer(FAR, 0)
    load_peer(RIGHT, 1)
    for i, k in ((0, LEFT), (1, RIGHT), (2, FAR)):
        pats[i].wait_recv()
        cp = near(pat_in.at[i], pat_s.at[k])
        cp.start()
        cp.wait()
    w_right.wait_recv()
    w_left.wait_recv()
    top, low = pl.ds(0, HALF), pl.ds(HALF, HALF)
    w_far = (
        remote(w_all.at[LEFT, top], w_all.at[FAR, top], xr),
        remote(w_all.at[RIGHT, low], w_all.at[FAR, low], xl),
    )
    for cp in w_far:
        cp.start()
    partial_unit(1)
    start_core(1)
    partial_unit(2)
    start_core(2)
    start_ring(1)
    tok_spread(LEFT)
    tok_spread(OWN)
    g_send.wait_recv()
    start_ring(2)
    partial_unit(3)
    start_core(3)
    step_ring(1)
    tok_forward(LEFT)
    weight_group(FAR, 0)
    d1 = (remote(dw.at[FAR, top], dx.at[0], xr), remote(dw.at[FAR, low], dx.at[1], xl))
    for cp in d1:
        cp.start()
    load_own(LEFT, 0)
    end_ring(1)
    step_ring(2)
    start_ring(3)
    tok_forward(OWN)
    tok_core(LEFT)
    weight_group(RIGHT, 1)
    load_own(OWN, 1)
    load_peer(LEFT, 0)
    dr = remote(dw.at[RIGHT, low], dx.at[2], xr)
    dr.start()
    to_owner(1)
    end_ring(2)
    step_ring(3)
    partial_unit(4)
    start_core(4)
    tok_core(OWN)
    weight_group(LEFT, 0)
    dl = remote(dw.at[LEFT, top], dx.at[3], xl)
    dl.start()
    load_peer(OWN, 1)
    start_ring(4)
    to_owner(2)
    end_ring(3)
    partial_unit(5)
    start_core(5)
    step_ring(4)
    to_owner(3)
    d1[0].wait_recv()
    add_rows(dw.at[RIGHT], 0, slice(None), [(dx.at[0], 0, slice(None))], HALF)
    d2r = remote(dw.at[RIGHT, top], dx.at[4], xr)
    d2r.start()
    d1[1].wait_recv()
    add_rows(dw.at[LEFT], HALF, slice(None), [(dx.at[1], 0, slice(None))], HALF)
    d2l = remote(dw.at[LEFT, low], dx.at[5], xl)
    d2l.start()
    start_ring(5)
    end_ring(4)
    for cp in w_far:
        cp.wait_recv()
    partial_unit(6)
    start_core(6)
    step_ring(5)
    to_owner(4)
    start_ring(6)
    partial_unit(7)
    start_core(7)
    end_ring(5)
    step_ring(6)
    start_ring(7)
    weight_group(OWN, 1)
    to_owner(5)
    end_ring(6)
    step_ring(7)
    to_owner(6)
    end_ring(7)
    to_owner(7)

    every = slice(None)

    def finish(row, first, second):
        def body(i, carry):
            here = pl.ds(pl.multiple_of(row + i * 16, 16), 16)
            there = pl.ds(pl.multiple_of(i * 16, 16), 16)
            total = dw[OWN, here, :].astype(jnp.float32) + dx[first, there, :].astype(jnp.float32)
            total = total + dx[second, there, :].astype(jnp.float32)
            gw_ref[here, :] = total.astype(jnp.bfloat16)
            return carry

        lax.fori_loop(0, HALF // 16, body, 0)

    dl.wait_recv()
    d2r.wait_recv()
    finish(0, 3, 4)
    dr.wait_recv()
    d2l.wait_recv()
    finish(HALF, 2, 5)
    pltpu.make_async_copy(gi_ref, gi_ref, local.at[0]).wait()

    for cp in sends:
        cp.wait_send()
    for cp, here in finals:
        if here is None:
            cp.wait_send()
        else:

            @pl.when(jnp.logical_not(here))
            def _():
                cp.wait_send()


N_REMOTE = 128
N_LOCAL = 24


def per_device(tokens, preact, grad_hidden, w_packed, block_cols, block_counts):
    pattern = jnp.concatenate([block_cols, block_counts], axis=1)
    pattern = jnp.pad(pattern, ((0, 16 - ROWS_DEV), (0, BLOCK - SLOTS - 1)))
    any_space = pl.BlockSpec(memory_space=pl.ANY)
    vmem = pl.BlockSpec(memory_space=pltpu.VMEM)
    bf16 = jnp.bfloat16
    grad_input, grad_weight, _ = pl.pallas_call(
        kernel,
        out_shape=(
            jax.ShapeDtypeStruct((PANEL, HALF), bf16),
            jax.ShapeDtypeStruct((WIDE, SLOTS * BLOCK), bf16),
            jax.ShapeDtypeStruct((4, PANEL, WIDE), bf16),
        ),
        in_specs=[vmem, any_space, any_space, any_space, any_space],
        out_specs=(any_space, vmem, any_space),
        scratch_shapes=[
            pltpu.VMEM((3, 16, BLOCK), jnp.int32),
            pltpu.SMEM((4, 16, BLOCK), jnp.int32),
            pltpu.VMEM((4, WIDE, SLOTS * BLOCK), bf16),
            pltpu.VMEM((COLS, PANEL, BLOCK), bf16),
            pltpu.VMEM((COLS, PANEL, BLOCK), bf16),
            pltpu.VMEM((2, 2, PANEL, WIDE), bf16),
            pltpu.VMEM((8, PANEL, WIDE), bf16),
            pltpu.VMEM((8, 256, WIDE), bf16),
            pltpu.VMEM((8, 6, 64, HALF), bf16),
            pltpu.VMEM((8, 32, WIDE), bf16),
            pltpu.VMEM((4, WIDE, SLOTS * BLOCK), bf16),
            pltpu.VMEM((6, HALF, SLOTS * BLOCK), bf16),
            pltpu.SemaphoreType.DMA((N_REMOTE,)),
            pltpu.SemaphoreType.DMA((N_REMOTE,)),
            pltpu.SemaphoreType.DMA((N_LOCAL,)),
        ],
        compiler_params=pltpu.CompilerParams(
            collective_id=0, has_side_effects=True, vmem_limit_bytes=60 << 20
        ),
        name="ffn_backward",
    )(pattern, tokens, preact, grad_hidden, w_packed)
    return grad_input, grad_weight


def solution(mesh):
    placed = (
        P("feat", None),
        P("feat", "hid"),
        P("feat", "hid"),
        P("feat", "hid"),
        P("feat", "hid"),
        P("feat", "hid"),
    )
    return jax.shard_map(
        per_device,
        mesh=mesh,
        in_specs=placed,
        out_specs=(P("feat", "hid"), P("feat", "hid")),
        check_vma=False,
    )
```

time: 451 us -> 174 us (0.39)
  the two profiles are of different devices: /device:TPU:2 before, /device:TPU:13 now
where the time goes in v1:
time: 174 us
  Pallas kernels  168 us (97%)
  local copies, waits for them, and re-layouts  5.45 us (3%)
    pallas_call x1, Pallas kernels, per_device(): pl.pallas_call(kernel, out_shape=(jax.ShapeDtypeStruct((PANEL, HALF), bf1...  168 us
    unnamed x6, local copies, waits for them, and re-layouts  4.84 us

profile of v1, /device:TPU:13, one launch (start us, length us, event | category | flops | bytes accessed | tf_op | source)
XLA Modules:
  0.0 174.1 jit_solution(15658927715221024979)
XLA Ops:
  0.6 0.8 copy.8
  1.4 0.7 copy.9
  2.1 0.1 pad_add_fusion
  2.2 0.6 pad.4.pat_ref
  2.8 167.9 %ffn_backward.1 = (bf16[512,768]{1,0:T(8,128)(2,1)}, bf16[1536,512]{1,0:T(8,128)(2,1)}, bf16[4,512,1536]{2,1,0:T(8,128)(2,1)}) custom-call(s32[16,128]{1,0:T(8,128)} %pad.4.pat_ref, bf16[512,12288]{1,0:T(8,128)(2,1)} %tokens.1, bf16[512,1536]{1,0:T(8,128)(2,1)} %preact.1, bf16[512,1536]{1,0:T(8,128)(2,1)} %grad_hidden.1, bf16[1536,512]{1,0:T(8,128)(2,1)} %w_hbm.1), custom_call_target="tpu_custom_call" | custom-call | tf_op jit(solution)/shard_map/ffn_backward/pallas_call | solution.py:458
  170.8 0.0 copy-start
  170.8 2.2 %copy.12 = bf16[512,768]{1,0:T(8,128)(2,1)} copy(bf16[512,768]{1,0:T(8,128)(2,1)} %get-tuple-element.8) | data formatting | bytes 1572864
  172.9 0.0 copy-done
  172.9 1.1 copy.13
Async XLA Ops:
  170.8 2.2 %copy-start = (bf16[1536,512]{1,0:T(8,128)(2,1)S(1)}, bf16[1536,512]{1,0:T(8,128)(2,1)}, u32[]{:S(2)}) copy-start(bf16[1536,512]{1,0:T(8,128)(2,1)} %get-tuple-element.9) | copy-start | bytes 4718596

commit v2 on v0

v2 whole, which is shorter than its diff:
```python
import functools

import jax
import jax.numpy as jnp
from jax import lax
from jax.experimental import pallas as pl
from jax.experimental.pallas import tpu as pltpu
from jax.sharding import PartitionSpec as P

BLOCK = 128
SLOTS = 4
PANEL = 512
ROWS_DEV = 12
WIDE = ROWS_DEV * BLOCK
HALF = WIDE // 2
COLS = 12
CUBIC = 0.044715
ROOT = 0.7978845608028654
MESH = pl.DeviceIdType.MESH
OWN, RIGHT, LEFT, FAR = 0, 1, 2, 3
X_STEP = (0, 1, 3, 2)
UNITS = (
    (0, OWN), (0, RIGHT), (0, LEFT), (0, FAR), (1, OWN), (1, RIGHT), (1, LEFT), (1, FAR),
)
UNROLL = 6


def gelu_slope(values):
    tangent = jnp.tanh(ROOT * (values + CUBIC * values * values * values))
    return 0.5 * (1.0 + tangent) + 0.5 * values * (1.0 - tangent * tangent) * ROOT * (
        1.0 + 3.0 * CUBIC * values * values
    )


def add_rows(dst, dst_row, dst_cols, terms, rows, step=32):
    def body(i, carry):
        off = i * step
        here = (pl.ds(pl.multiple_of(dst_row + off, 16), step), dst_cols)
        total = dst[here].astype(jnp.float32)
        for ref, row, cols in terms:
            total = total + ref[pl.ds(pl.multiple_of(row + off, 16), step), cols].astype(jnp.float32)
        dst[here] = total.astype(jnp.bfloat16)
        return carry

    lax.fori_loop(0, rows // step, body, 0)


def kernel(
    pat_ref, tokens, preact, grad_hidden, w_hbm,
    gi_ref, gw_ref, tp_ref,
    pat_in, pat_s, w_all, g_own, g_peer, tok_s, part, rb1, r2, rb3, dw, dx,
    send, recv, local,
):
    f, h = lax.axis_index("feat"), lax.axis_index("hid")
    x, zh, zl, y, c = f // 2, f % 2, h // 8, (h // 2) % 4, h % 2

    def dev(x_, zh_, zl_, y_, c_):
        return (x_ * 2 + zh_, zl_ * 8 + y_ * 2 + c_)

    xg = [(x + s) % 4 for s in X_STEP]
    core = dev(x, zh, zl, y, 1 - c)
    xr, xl, xo = dev(xg[RIGHT], zh, zl, y, c), dev(xg[LEFT], zh, zl, y, c), dev(xg[FAR], zh, zl, y, c)
    yr, yl = dev(x, zh, zl, (y + 1) % 4, c), dev(x, zh, zl, (y + 3) % 4, c)
    zlp, zhp = dev(x, zh, 1 - zl, y, c), dev(x, 1 - zh, zl, y, c)

    count = {"remote": 0, "local": 1}
    sends = []
    moving = {}

    def remote(name, src, dst, device):
        i = count["remote"]
        count["remote"] += 1
        cp = pltpu.make_async_remote_copy(
            src_ref=src, dst_ref=dst, send_sem=send.at[i], recv_sem=recv.at[i],
            device_id=device, device_id_type=MESH,
        )
        cp.start()
        sends.append(cp)
        moving[name] = cp.wait_recv

    def near(name, src, dst):
        i = count["local"]
        count["local"] += 1
        cp = pltpu.make_async_copy(src, dst, local.at[i])
        cp.start()
        moving[name] = cp.wait

    def need(*names):
        for name in names:
            wait = moving.get(name)
            if wait is not None:
                wait()
            moving[name] = None

    near("preact", preact, part.at[6])
    near("grad", grad_hidden, part.at[7])
    near(("w", OWN), w_hbm, w_all.at[OWN])
    near(("pat", OWN), pat_ref, pat_s.at[OWN])

    barrier = pltpu.get_barrier_semaphore()

    def greet(device):
        pl.semaphore_signal(barrier, inc=1, device_id=device, device_id_type=MESH)

    for device in (core, xr, xl, xo, yr, yl, zlp, zhp):
        greet(device)
    mine = (y % 2) == zh
    for other in range(8):
        other_y, other_c = other // 2, other % 2
        skip = jnp.logical_and(mine, jnp.logical_and(y == other_y, c == other_c))

        @pl.when(jnp.logical_not(skip))
        def _():
            greet(dev(x, y % 2, zl, other_y, other_c))

    pl.semaphore_wait(barrier, 16 - mine.astype(jnp.int32))

    def start_patterns():
        for i, (k, device) in enumerate(((LEFT, xr), (RIGHT, xl), (FAR, xo))):
            remote(("pat", k), pat_ref, pat_in.at[i], device)

    def start_weights():
        remote(("w", LEFT), w_hbm, w_all.at[LEFT], xr)
        remote(("w", RIGHT), w_hbm, w_all.at[RIGHT], xl)

    def patterns():
        for i, k in enumerate((LEFT, RIGHT, FAR)):
            need(("pat", k))
            near(("pat in", k), pat_in.at[i], pat_s.at[k])
        for k in (LEFT, RIGHT, FAR):
            need(("pat in", k))
        need(("w", OWN), ("pat", OWN))

    top, low = pl.ds(0, HALF), pl.ds(HALF, HALF)

    def forward_weights():
        need(("w", LEFT), ("w", RIGHT))
        remote(("w", FAR), w_all.at[LEFT, top], w_all.at[FAR, top], xr)
        remote("w far low", w_all.at[RIGHT, low], w_all.at[FAR, low], xl)

    piece = pl.multiple_of(c * 256 + y * 64, 64)
    every = slice(None)

    def rows_of(at, n):
        return pl.ds(pl.multiple_of(at, 16), n)

    def group_cols(k, zh_):
        return pl.ds(pl.multiple_of((2 * xg[k] + zh_) * WIDE, 128), WIDE)

    def tok0(k):
        rows = pl.ds(piece, 64)
        remote(("t0", k), tokens.at[rows, group_cols(k, 1 - zh)], tp_ref.at[k, rows], zhp)

    def gelu(half):
        need("preact", "grad")
        cols = pl.ds(half * HALF, HALF)

        def slope_step(i, carry):
            rows = pl.ds(pl.multiple_of(i * 16, 16), 16)
            value = part[6, rows, cols].astype(jnp.float32)
            grad = (part[7, rows, cols].astype(jnp.float32) * gelu_slope(value)).astype(jnp.bfloat16)
            for b in range(COLS // 2):
                g_own[half * COLS // 2 + b, rows, :] = grad[:, b * BLOCK:(b + 1) * BLOCK]
            return carry

        lax.fori_loop(0, PANEL // 16, slope_step, 0)
        blocks = pl.ds(half * COLS // 2, COLS // 2)
        remote(("g", half), g_own.at[blocks], g_peer.at[blocks], zhp)

    def selected(panel, k, r, rows):
        grad = (g_own, g_peer)[panel]
        return jnp.concatenate([grad[pat_s[k, r, s], rows, :] for s in range(SLOTS)], axis=1)

    def live(k, r):
        lanes = lax.broadcasted_iota(jnp.int32, (BLOCK, SLOTS * BLOCK), 1)
        return lanes < pat_s[k, r, SLOTS] * BLOCK

    def each_row(body):
        def several(i, carry):
            for v in range(UNROLL):
                r = UNROLL * i + v
                body(r, pl.ds(pl.multiple_of(r * BLOCK, BLOCK), BLOCK))
            return carry

        lax.fori_loop(0, ROWS_DEV // UNROLL, several, 0)

    def partial_half(u, rows, extra):
        panel, k = UNITS[u]
        if panel == 1:
            need(("g", 0), ("g", 1))
        if k == FAR:
            need(("w", FAR), "w far low")

        def body(r, at):
            weights = jnp.where(live(k, r), w_all[k, at, :], jnp.zeros((), jnp.bfloat16))
            total = lax.dot_general(
                selected(panel, k, r, rows), weights, (((1,), (1,)), ((), ())),
                preferred_element_type=jnp.float32,
            )
            if extra:
                total = total + rb1[u, :, at].astype(jnp.float32)
            part[u, rows, at] = total.astype(jnp.bfloat16)

        each_row(body)

    A, B = pl.ds(0, HALF), pl.ds(HALF, HALF)

    def chunk(t):
        return pl.multiple_of(c * 256 + ((y + t) % 4) * 64, 64)

    def first(u):
        rows = rows_of((1 - c) * 256, 256)
        partial_half(u, rows, False)
        remote(("core", u), part.at[u, rows], rb1.at[u], core)

    def second(u):
        need(("core", u))
        partial_half(u, rows_of(c * 256, 256), True)
        remote(("r0", u), part.at[u, rows_of(chunk(2), 64), A], r2.at[u, 0], yr)
        remote(("r1", u), part.at[u, rows_of(chunk(2), 64), B], r2.at[u, 1], yl)
        remote(("r2", u), part.at[u, rows_of(chunk(1), 64), B], r2.at[u, 2], yr)
        remote(("r3", u), part.at[u, rows_of(chunk(3), 64), A], r2.at[u, 3], yl)

    def step_right(u):
        need(("r0", u))
        add_rows(part.at[u], chunk(1), A, [(r2.at[u, 0], 0, every)], 64)
        remote(("r4", u), part.at[u, rows_of(chunk(1), 64), A], r2.at[u, 4], yr)

    def step_left(u):
        need(("r1", u))
        add_rows(part.at[u], chunk(3), B, [(r2.at[u, 1], 0, every)], 64)
        remote(("r5", u), part.at[u, rows_of(chunk(3), 64), B], r2.at[u, 5], yl)

    finals = []
    crossing = {}

    def end_ring(u):
        need(("r3", u), ("r4", u))
        add_rows(part.at[u], chunk(0), A, [(r2.at[u, 3], 0, every), (r2.at[u, 4], 0, every)], 64)
        need(("r2", u), ("r5", u))
        add_rows(part.at[u], chunk(0), B, [(r2.at[u, 2], 0, every), (r2.at[u, 5], 0, every)], 64)
        stays = xg[UNITS[u][1]] // 2 == zl
        i = count["remote"]
        count["remote"] += 1
        cp = pltpu.make_async_remote_copy(
            src_ref=part.at[u, rows_of(chunk(0), 64)], dst_ref=rb3.at[u],
            send_sem=send.at[i], recv_sem=recv.at[i], device_id=zlp, device_id_type=MESH,
        )

        @pl.when(jnp.logical_not(stays))
        def _():
            cp.start()

        finals.append((cp, jnp.logical_not(stays)))
        crossing[u] = cp, stays


    def to_owner(u):
        panel, k = UNITS[u]
        cp3, stays = crossing[u]

        @pl.when(stays)
        def _():
            cp3.wait_recv()
            add_rows(part.at[u], chunk(0), every, [(rb3.at[u], 0, every)], 64)

        for j, cols in enumerate((A, B)):
            owner = dev(x, zh if panel == 0 else 1 - zh, zl, (xg[k] % 2) * 2 + zh, j)
            src = part.at[u, rows_of(chunk(0), 64), cols]
            dst = gi_ref.at[rows_of(chunk(0), 64)]
            i = count["remote"]
            count["remote"] += 1
            cp = pltpu.make_async_remote_copy(
                src_ref=src, dst_ref=dst, send_sem=send.at[i], recv_sem=local.at[0],
                device_id=owner, device_id_type=MESH,
            )
            away = stays
            if panel == 0:
                here = jnp.logical_and(owner[1] == h, stays)
                away = jnp.logical_and(owner[1] != h, stays)
                stay = pltpu.make_async_copy(src, dst, local.at[0])

                @pl.when(here)
                def _():
                    stay.start()

            @pl.when(away)
            def _():
                cp.start()

            finals.append((cp, away))

    def spread(k):
        need(("t0", k))
        at = tp_ref.at[k, pl.ds(piece, 64)]
        remote(("t1r", k), at, at, yr)
        remote(("t1l", k), at, at, yl)

    def forward_right(k):
        need(("t1r", k))
        at = tp_ref.at[k, rows_of(chunk(3), 32)]
        remote(("t2r", k), at, at, yr)

    def forward_left(k):
        need(("t1l", k))
        at = tp_ref.at[k, rows_of(chunk(1) + 32, 32)]
        remote(("t2l", k), at, at, yl)

    def tok_core(k):
        need(("t2r", k), ("t2l", k))
        at = tp_ref.at[k, rows_of(c * 256, 256)]
        remote(("t3", k), at, at, core)

    def load_own(k):
        near(("lo", k), tokens.at[:, group_cols(k, zh)], tok_s.at[k])

    def load_peer(k):
        need(("t3", k))
        near(("lp", k), tp_ref.at[k], tok_s.at[k])

    def weight_term(k, panel):
        def body(r, at):
            total = lax.dot_general(
                tok_s[k, :, at], selected(panel, k, r, every), (((0,), (0,)), ((), ())),
                preferred_element_type=jnp.float32,
            )
            total = jnp.where(live(k, r), total, 0.0)
            if panel == 1:
                total = total + dw[k, at, :].astype(jnp.float32)
            dw[k, at, :] = total.astype(jnp.bfloat16)

        each_row(body)

    def term_own(k):
        need(("lo", k))
        weight_term(k, 0)

    def term_peer(k):
        need(("lp", k), ("g", 0), ("g", 1))
        weight_term(k, 1)
        if k == FAR:
            remote("d1r", dw.at[FAR, top], dx.at[0], xr)
            remote("d1l", dw.at[FAR, low], dx.at[1], xl)
        if k == RIGHT:
            remote("dr", dw.at[RIGHT, low], dx.at[2], xr)
        if k == LEFT:
            remote("dl", dw.at[LEFT, top], dx.at[3], xl)

    def pass_right():
        need("d1r")
        add_rows(dw.at[RIGHT], 0, every, [(dx.at[0], 0, every)], HALF)
        remote("d2r", dw.at[RIGHT, top], dx.at[4], xr)

    def pass_left():
        need("d1l")
        add_rows(dw.at[LEFT], HALF, every, [(dx.at[1], 0, every)], HALF)
        remote("d2l", dw.at[LEFT, low], dx.at[5], xl)

    def finish(row, first_, second_):
        def body(i, carry):
            here = pl.ds(pl.multiple_of(row + i * 32, 32), 32)
            there = pl.ds(pl.multiple_of(i * 32, 32), 32)
            total = dw[OWN, here, :].astype(jnp.float32) + dx[first_, there, :].astype(jnp.float32)
            total = total + dx[second_, there, :].astype(jnp.float32)
            gw_ref[here, :] = total.astype(jnp.bfloat16)
            return carry

        lax.fori_loop(0, HALF // 32, body, 0)

    start_patterns()
    start_weights()
    tok0(FAR)
    tok0(RIGHT)
    tok0(LEFT)
    tok0(OWN)
    load_own(FAR)
    load_own(RIGHT)
    load_own(LEFT)
    load_own(OWN)
    gelu(0)
    gelu(1)
    patterns()
    spread(FAR)
    first(0)
    term_own(FAR)
    term_own(RIGHT)
    spread(RIGHT)
    second(0)
    forward_right(FAR)
    forward_left(FAR)
    term_own(LEFT)
    term_own(OWN)
    spread(LEFT)
    forward_right(RIGHT)
    forward_left(RIGHT)
    step_right(0)
    step_left(0)
    spread(OWN)
    tok_core(FAR)
    load_peer(FAR)
    forward_weights()
    forward_right(LEFT)
    forward_left(LEFT)
    tok_core(RIGHT)
    end_ring(0)
    load_peer(RIGHT)
    forward_right(OWN)
    forward_left(OWN)
    first(1)
    first(2)
    tok_core(LEFT)
    second(1)
    tok_core(OWN)
    second(2)
    load_peer(LEFT)
    load_peer(OWN)
    step_right(1)
    step_left(1)
    step_right(2)
    step_left(2)
    end_ring(1)
    term_peer(FAR)
    term_peer(RIGHT)
    term_peer(LEFT)
    term_peer(OWN)
    to_owner(0)
    end_ring(2)
    first(3)
    first(4)
    to_owner(1)
    first(5)
    second(3)
    to_owner(2)
    second(4)
    second(5)
    step_right(3)
    step_left(3)
    first(6)
    second(6)
    pass_right()
    pass_left()
    step_right(4)
    step_left(4)
    step_right(5)
    step_left(5)
    end_ring(3)
    first(7)
    step_right(6)
    step_left(6)
    second(7)
    to_owner(3)
    end_ring(4)
    end_ring(5)
    end_ring(6)
    to_owner(4)
    step_right(7)
    step_left(7)
    to_owner(5)
    to_owner(6)
    end_ring(7)
    to_owner(7)
    need("dl", "d2r")
    finish(0, 3, 4)
    need("dr", "d2l")
    finish(HALF, 2, 5)
    need(*moving)
    if any(started is not None for _, started in finals):
        pltpu.make_async_copy(gi_ref, gi_ref, local.at[0]).wait()

    for cp in sends:
        cp.wait_send()
    for cp, started in finals:

        @pl.when(started)
        def _():
            cp.wait_send()


N_REMOTE = 136
N_LOCAL = 24


def per_device(tokens, preact, grad_hidden, w_packed, block_cols, block_counts):
    pattern = jnp.concatenate([block_cols, block_counts], axis=1)
    pattern = jnp.pad(pattern, ((0, 16 - ROWS_DEV), (0, BLOCK - SLOTS - 1)))
    any_space = pl.BlockSpec(memory_space=pl.ANY)
    vmem = pl.BlockSpec(memory_space=pltpu.VMEM)
    bf16 = jnp.bfloat16
    grad_input, grad_weight, _ = pl.pallas_call(
        kernel,
        out_shape=(
            jax.ShapeDtypeStruct((PANEL, HALF), bf16),
            jax.ShapeDtypeStruct((WIDE, SLOTS * BLOCK), bf16),
            jax.ShapeDtypeStruct((4, PANEL, WIDE), bf16),
        ),
        in_specs=[vmem] + [any_space] * 4,
        out_specs=(any_space, vmem, any_space),
        scratch_shapes=[
            pltpu.VMEM((3, 16, BLOCK), jnp.int32),
            pltpu.SMEM((4, 16, BLOCK), jnp.int32),
            pltpu.VMEM((4, WIDE, SLOTS * BLOCK), bf16),
            pltpu.VMEM((COLS, PANEL, BLOCK), bf16),
            pltpu.VMEM((COLS, PANEL, BLOCK), bf16),
            pltpu.VMEM((4, PANEL, WIDE), bf16),
            pltpu.VMEM((8, PANEL, WIDE), bf16),
            pltpu.VMEM((8, 256, WIDE), bf16),
            pltpu.VMEM((8, 6, 64, HALF), bf16),
            pltpu.VMEM((8, 64, WIDE), bf16),
            pltpu.VMEM((4, WIDE, SLOTS * BLOCK), bf16),
            pltpu.VMEM((6, HALF, SLOTS * BLOCK), bf16),
            pltpu.SemaphoreType.DMA((N_REMOTE,)),
            pltpu.SemaphoreType.DMA((N_REMOTE,)),
            pltpu.SemaphoreType.DMA((N_LOCAL,)),
        ],
        compiler_params=pltpu.CompilerParams(
            collective_id=0, has_side_effects=True, vmem_limit_bytes=60 << 20
        ),
        name="ffn_backward",
    )(pattern, tokens, preact, grad_hidden, w_packed)
    return grad_input, grad_weight


def solution(mesh):
    placed = (
        P("feat", None),
        P("feat", "hid"),
        P("feat", "hid"),
        P("feat", "hid"),
        P("feat", "hid"),
        P("feat", "hid"),
    )
    return jax.shard_map(
        per_device,
        mesh=mesh,
        in_specs=placed,
        out_specs=(P("feat", "hid"), P("feat", "hid")),
        check_vma=False,
    )
```

time: 451 us -> 154 us (0.34)
  the two profiles are of different devices: /device:TPU:2 before, /device:TPU:97 now
where the time goes in v2:
time: 154 us
  Pallas kernels  148 us (96%)
  local copies, waits for them, and re-layouts  5.45 us (4%)
    pallas_call x1, Pallas kernels, per_device(): pl.pallas_call(kernel, out_shape=(jax.ShapeDtypeStruct((PANEL, HALF), bf1...  148 us
    unnamed x6, local copies, waits for them, and re-layouts  4.84 us

profile of v2, /device:TPU:97, one launch (start us, length us, event | category | flops | bytes accessed | tf_op | source)
XLA Modules:
  0.0 154.0 jit_solution(5878138103114818350)
XLA Ops:
  0.6 0.8 copy.8
  1.4 0.7 copy.9
  2.1 0.1 pad_add_fusion
  2.2 0.6 pad.4.pat_ref
  2.8 147.9 %ffn_backward.1 = (bf16[512,768]{1,0:T(8,128)(2,1)}, bf16[1536,512]{1,0:T(8,128)(2,1)}, bf16[4,512,1536]{2,1,0:T(8,128)(2,1)}) custom-call(s32[16,128]{1,0:T(8,128)} %pad.4.pat_ref, bf16[512,12288]{1,0:T(8,128)(2,1)} %tokens.1, bf16[512,1536]{1,0:T(8,128)(2,1)} %preact.1, bf16[512,1536]{1,0:T(8,128)(2,1)} %grad_hidden.1, bf16[1536,512]{1,0:T(8,128)(2,1)} %w_hbm.1), custom_call_target="tpu_custom_call" | custom-call | tf_op jit(solution)/shard_map/ffn_backward/pallas_call | solution.py:489
  150.7 0.0 copy-start
  150.7 2.2 %copy.12 = bf16[512,768]{1,0:T(8,128)(2,1)} copy(bf16[512,768]{1,0:T(8,128)(2,1)} %get-tuple-element.8) | data formatting | bytes 1572864
  152.9 0.0 copy-done
  152.9 1.1 copy.13
Async XLA Ops:
  150.7 2.2 %copy-start = (bf16[1536,512]{1,0:T(8,128)(2,1)S(1)}, bf16[1536,512]{1,0:T(8,128)(2,1)}, u32[]{:S(2)}) copy-start(bf16[1536,512]{1,0:T(8,128)(2,1)} %get-tuple-element.9) | copy-start | bytes 4718596

commit v3 on v2

--- a/solution.py
+++ b/solution.py
@@ -105,15 +105,20 @@
     for device in (core, xr, xl, xo, yr, yl, zlp, zhp):
         greet(device)
     mine = (y % 2) == zh
-    for other in range(8):
-        other_y, other_c = other // 2, other % 2
-        skip = jnp.logical_and(mine, jnp.logical_and(y == other_y, c == other_c))
-
-        @pl.when(jnp.logical_not(skip))
-        def _():
-            greet(dev(x, y % 2, zl, other_y, other_c))
-
-    pl.semaphore_wait(barrier, 16 - mine.astype(jnp.int32))
+    side = jnp.where(c == zl, y, (y + 3 + 2 * zl) % 4)
+    for t in range(4):
+        for other_c in range(2):
+            if t == 0:
+                sends_here = jnp.logical_not(jnp.logical_and(mine, c == other_c))
+                other_y = jnp.where(mine, y, side)
+            else:
+                sends_here, other_y = mine, (y + t) % 4
+
+            @pl.when(sends_here)
+            def _():
+                greet(dev(x, y % 2, zl, other_y, other_c))
+
+    pl.semaphore_wait(barrier, 13 - mine.astype(jnp.int32))
 
     def start_patterns():
         for i, (k, device) in enumerate(((LEFT, xr), (RIGHT, xl), (FAR, xo))):
@@ -216,34 +221,63 @@
     def second(u):
         need(("core", u))
         partial_half(u, rows_of(c * 256, 256), True)
-        remote(("r0", u), part.at[u, rows_of(chunk(2), 64), A], r2.at[u, 0], yr)
-        remote(("r1", u), part.at[u, rows_of(chunk(2), 64), B], r2.at[u, 1], yl)
-        remote(("r2", u), part.at[u, rows_of(chunk(1), 64), B], r2.at[u, 2], yr)
-        remote(("r3", u), part.at[u, rows_of(chunk(3), 64), A], r2.at[u, 3], yl)
+        if u < 4:
+            ring(u)
+
+    def share(u, t, half):
+        if u < 4:
+            return part.at[u], chunk(t)
+        turn = (y + t - zh) % 4
+        group = jnp.where(
+            half == 0, (turn % 2) * 2 + turn // 2,
+            jnp.where(turn % 2 == 0, 2 + turn // 2, 1 - turn // 2),
+        )
+        step = (group - x) % 4
+        index = jnp.where(step == 2, FAR, jnp.where(step == 3, LEFT, step))
+        return part.at[4 + index], pl.multiple_of(c * 256 + (u - 4) * 64, 64)
+
+    def share_at(u, t, half):
+        ref, row = share(u, t, half)
+        return ref.at[pl.ds(row, 64), pl.ds(pl.multiple_of(half * HALF, 128), HALF)]
+
+    def ring(u):
+        remote(("r0", u), share_at(u, 2, 0), r2.at[u, 0], yr)
+        remote(("r1", u), share_at(u, 2, 1), r2.at[u, 1], yl)
+        remote(("r2", u), share_at(u, 1, 1), r2.at[u, 2], yr)
+        remote(("r3", u), share_at(u, 3, 0), r2.at[u, 3], yl)
 
     def step_right(u):
         need(("r0", u))
-        add_rows(part.at[u], chunk(1), A, [(r2.at[u, 0], 0, every)], 64)
-        remote(("r4", u), part.at[u, rows_of(chunk(1), 64), A], r2.at[u, 4], yr)
+        ref, row = share(u, 1, 0)
+        add_rows(ref, row, A, [(r2.at[u, 0], 0, every)], 64)
+        remote(("r4", u), share_at(u, 1, 0), r2.at[u, 4], yr)
 
     def step_left(u):
         need(("r1", u))
-        add_rows(part.at[u], chunk(3), B, [(r2.at[u, 1], 0, every)], 64)
-        remote(("r5", u), part.at[u, rows_of(chunk(3), 64), B], r2.at[u, 5], yl)
+        ref, row = share(u, 3, 1)
+        add_rows(ref, row, B, [(r2.at[u, 1], 0, every)], 64)
+        remote(("r5", u), share_at(u, 3, 1), r2.at[u, 5], yl)
 
     finals = []
     crossing = {}
+    odd = (y - zh) % 2
+    kept = (odd + zl) % 2
 
     def end_ring(u):
         need(("r3", u), ("r4", u))
-        add_rows(part.at[u], chunk(0), A, [(r2.at[u, 3], 0, every), (r2.at[u, 4], 0, every)], 64)
+        ref, row = share(u, 0, 0)
+        add_rows(ref, row, A, [(r2.at[u, 3], 0, every), (r2.at[u, 4], 0, every)], 64)
         need(("r2", u), ("r5", u))
-        add_rows(part.at[u], chunk(0), B, [(r2.at[u, 2], 0, every), (r2.at[u, 5], 0, every)], 64)
+        ref, row = share(u, 0, 1)
+        add_rows(ref, row, B, [(r2.at[u, 2], 0, every), (r2.at[u, 5], 0, every)], 64)
+        if u >= 4:
+            remote(("zl", u), share_at(u, 0, 1 - kept), rb3.at[u, :, A], zlp)
+            return
         stays = xg[UNITS[u][1]] // 2 == zl
         i = count["remote"]
         count["remote"] += 1
         cp = pltpu.make_async_remote_copy(
-            src_ref=part.at[u, rows_of(chunk(0), 64)], dst_ref=rb3.at[u],
+            src_ref=part.at[u, pl.ds(chunk(0), 64)], dst_ref=rb3.at[u],
             send_sem=send.at[i], recv_sem=recv.at[i], device_id=zlp, device_id_type=MESH,
         )
 
@@ -257,6 +291,22 @@
 
     def to_owner(u):
         panel, k = UNITS[u]
+        if panel == 1:
+            need(("zl", u))
+            ref, row = share(u, 0, kept)
+            cols = pl.ds(pl.multiple_of(kept * HALF, 128), HALF)
+            add_rows(ref, row, cols, [(rb3.at[u], 0, A)], 64)
+            i = count["remote"]
+            count["remote"] += 1
+            cp = pltpu.make_async_remote_copy(
+                src_ref=share_at(u, 0, kept), dst_ref=gi_ref.at[pl.ds(row, 64)],
+                send_sem=send.at[i], recv_sem=local.at[0],
+                device_id=dev(x, 1 - zh, zl, (y + 4 + odd * (2 * kept - 1)) % 4, kept),
+                device_id_type=MESH,
+            )
+            cp.start()
+            sends.append(cp)
+            return
         cp3, stays = crossing[u]
 
         @pl.when(stays)
@@ -265,24 +315,22 @@
             add_rows(part.at[u], chunk(0), every, [(rb3.at[u], 0, every)], 64)
 
         for j, cols in enumerate((A, B)):
-            owner = dev(x, zh if panel == 0 else 1 - zh, zl, (xg[k] % 2) * 2 + zh, j)
-            src = part.at[u, rows_of(chunk(0), 64), cols]
-            dst = gi_ref.at[rows_of(chunk(0), 64)]
+            owner = dev(x, zh, zl, (xg[k] % 2) * 2 + zh, j)
+            src = part.at[u, pl.ds(chunk(0), 64), cols]
+            dst = gi_ref.at[pl.ds(chunk(0), 64)]
             i = count["remote"]
             count["remote"] += 1
             cp = pltpu.make_async_remote_copy(
                 src_ref=src, dst_ref=dst, send_sem=send.at[i], recv_sem=local.at[0],
                 device_id=owner, device_id_type=MESH,
             )
-            away = stays
-            if panel == 0:
-                here = jnp.logical_and(owner[1] == h, stays)
-                away = jnp.logical_and(owner[1] != h, stays)
-                stay = pltpu.make_async_copy(src, dst, local.at[0])
-
-                @pl.when(here)
-                def _():
-                    stay.start()
+            here = jnp.logical_and(owner[1] == h, stays)
+            away = jnp.logical_and(owner[1] != h, stays)
+            stay = pltpu.make_async_copy(src, dst, local.at[0])
+
+            @pl.when(here)
+            def _():
+                stay.start()
 
             @pl.when(away)
             def _():
@@ -380,91 +428,95 @@
     gelu(0)
     gelu(1)
     patterns()
+    first(0)
     spread(FAR)
-    first(0)
     term_own(FAR)
     term_own(RIGHT)
+    term_own(LEFT)
     spread(RIGHT)
     second(0)
+    term_own(OWN)
     forward_right(FAR)
     forward_left(FAR)
-    term_own(LEFT)
-    term_own(OWN)
     spread(LEFT)
     forward_right(RIGHT)
     forward_left(RIGHT)
+    spread(OWN)
     step_right(0)
     step_left(0)
-    spread(OWN)
     tok_core(FAR)
     load_peer(FAR)
-    forward_weights()
     forward_right(LEFT)
     forward_left(LEFT)
     tok_core(RIGHT)
-    end_ring(0)
     load_peer(RIGHT)
+    forward_weights()
     forward_right(OWN)
     forward_left(OWN)
     first(1)
-    first(2)
+    end_ring(0)
     tok_core(LEFT)
     second(1)
     tok_core(OWN)
-    second(2)
+    first(2)
     load_peer(LEFT)
     load_peer(OWN)
     step_right(1)
     step_left(1)
+    second(2)
+    end_ring(1)
     step_right(2)
     step_left(2)
-    end_ring(1)
     term_peer(FAR)
     term_peer(RIGHT)
-    term_peer(LEFT)
-    term_peer(OWN)
-    to_owner(0)
+    first(3)
     end_ring(2)
-    first(3)
     first(4)
-    to_owner(1)
+    second(3)
     first(5)
-    second(3)
-    to_owner(2)
+    first(6)
     second(4)
+    first(7)
     second(5)
+    second(6)
     step_right(3)
     step_left(3)
-    first(6)
-    second(6)
+    second(7)
+    ring(4)
+    ring(5)
+    term_peer(LEFT)
+    step_right(4)
+    step_left(4)
+    ring(6)
     pass_right()
     pass_left()
-    step_right(4)
-    step_left(4)
     step_right(5)
     step_left(5)
+    ring(7)
+    term_peer(OWN)
     end_ring(3)
-    first(7)
+    end_ring(4)
     step_right(6)
     step_left(6)
-    second(7)
-    to_owner(3)
-    end_ring(4)
     end_ring(5)
+    step_right(7)
+    step_left(7)
     end_ring(6)
     to_owner(4)
-    step_right(7)
-    step_left(7)
     to_owner(5)
+    end_ring(7)
+    to_owner(0)
+    to_owner(1)
+    to_owner(2)
+    to_owner(3)
     to_owner(6)
-    end_ring(7)
     to_owner(7)
     need("dl", "d2r")
     finish(0, 3, 4)
     need("dr", "d2l")
     finish(HALF, 2, 5)
     need(*moving)
-    if any(started is not None for _, started in finals):
+    if finals:
         pltpu.make_async_copy(gi_ref, gi_ref, local.at[0]).wait()
 
     for cp in sends:

time: 154 us -> 135 us (0.88)
  the two profiles are of different devices: /device:TPU:97 before, /device:TPU:2 now
where the time goes in v3:
time: 135 us; the launch traced here: 134 us
  Pallas kernels  128 us (95%)
  local copies, waits for them, and re-layouts  5.45 us (4%)
    pallas_call x1, Pallas kernels, per_device(): pl.pallas_call(kernel, out_shape=(jax.ShapeDtypeStruct((PANEL, HALF), bf1...  128 us
    unnamed x6, local copies, waits for them, and re-layouts  4.84 us

profile of v3, /device:TPU:2, one launch (start us, length us, event | category | flops | bytes accessed | tf_op | source)
XLA Modules:
  0.0 133.7 jit_solution(1769224181697419562)
XLA Ops:
  0.6 0.8 copy.8
  1.4 0.7 copy.9
  2.1 0.1 pad_add_fusion
  2.2 0.6 pad.4.pat_ref
  2.8 127.6 %ffn_backward.1 = (bf16[512,768]{1,0:T(8,128)(2,1)}, bf16[1536,512]{1,0:T(8,128)(2,1)}, bf16[4,512,1536]{2,1,0:T(8,128)(2,1)}) custom-call(s32[16,128]{1,0:T(8,128)} %pad.4.pat_ref, bf16[512,12288]{1,0:T(8,128)(2,1)} %tokens.1, bf16[512,1536]{1,0:T(8,128)(2,1)} %preact.1, bf16[512,1536]{1,0:T(8,128)(2,1)} %grad_hidden.1, bf16[1536,512]{1,0:T(8,128)(2,1)} %w_hbm.1), custom_call_target="tpu_custom_call" | custom-call | tf_op jit(solution)/shard_map/ffn_backward/pallas_call | solution.py:541
  130.4 0.0 copy-start
  130.4 2.2 %copy.12 = bf16[512,768]{1,0:T(8,128)(2,1)} copy(bf16[512,768]{1,0:T(8,128)(2,1)} %get-tuple-element.8) | data formatting | bytes 1572864
  132.6 0.0 copy-done
  132.6 1.1 copy.13
Async XLA Ops:
  130.4 2.2 %copy-start = (bf16[1536,512]{1,0:T(8,128)(2,1)S(1)}, bf16[1536,512]{1,0:T(8,128)(2,1)}, u32[]{:S(2)}) copy-start(bf16[1536,512]{1,0:T(8,128)(2,1)} %get-tuple-element.9) | copy-start | bytes 4718596

commit v4 on v3

--- a/solution.py
+++ b/solution.py
@@ -46,9 +46,9 @@
 
 
 def kernel(
-    pat_ref, tokens, preact, grad_hidden, w_hbm,
+    cols_ref, counts_ref, tokens, preact, grad_hidden, w_hbm,
     gi_ref, gw_ref, tp_ref,
-    pat_in, pat_s, w_all, g_own, g_peer, tok_s, part, rb1, r2, rb3, dw, dx,
+    pat_ref, pat_in, pat_s, w_all, g_own, g_peer, tok_s, part, rb1, r2, rb3, rb4, dw, dx,
     send, recv, local,
 ):
     f, h = lax.axis_index("feat"), lax.axis_index("hid")
@@ -95,6 +95,9 @@
     near("preact", preact, part.at[6])
     near("grad", grad_hidden, part.at[7])
     near(("w", OWN), w_hbm, w_all.at[OWN])
+    pat_ref[...] = jnp.zeros_like(pat_ref)
+    pat_ref[:SLOTS, :ROWS_DEV] = cols_ref[...]
+    pat_ref[SLOTS:SLOTS + 1, :ROWS_DEV] = counts_ref[...]
     near(("pat", OWN), pat_ref, pat_s.at[OWN])
 
     barrier = pltpu.get_barrier_semaphore()
@@ -108,17 +111,19 @@
     side = jnp.where(c == zl, y, (y + 3 + 2 * zl) % 4)
     for t in range(4):
         for other_c in range(2):
+            other_y = (y + t) % 4
             if t == 0:
-                sends_here = jnp.logical_not(jnp.logical_and(mine, c == other_c))
                 other_y = jnp.where(mine, y, side)
+                sends_here = jnp.logical_not(jnp.logical_and(other_y == y, c == other_c))
             else:
-                sends_here, other_y = mine, (y + t) % 4
+                sends_here = mine
 
             @pl.when(sends_here)
             def _():
-                greet(dev(x, y % 2, zl, other_y, other_c))
-
-    pl.semaphore_wait(barrier, 13 - mine.astype(jnp.int32))
+                greet(dev(x, zh, zl, other_y, other_c))
+
+    stay_put = jnp.logical_and(jnp.logical_not(mine), c == zl)
+    pl.semaphore_wait(barrier, 13 - mine.astype(jnp.int32) - stay_put.astype(jnp.int32))
 
     def start_patterns():
         for i, (k, device) in enumerate(((LEFT, xr), (RIGHT, xl), (FAR, xo))):
@@ -174,11 +179,11 @@
 
     def selected(panel, k, r, rows):
         grad = (g_own, g_peer)[panel]
-        return jnp.concatenate([grad[pat_s[k, r, s], rows, :] for s in range(SLOTS)], axis=1)
+        return jnp.concatenate([grad[pat_s[k, s, r], rows, :] for s in range(SLOTS)], axis=1)
 
     def live(k, r):
         lanes = lax.broadcasted_iota(jnp.int32, (BLOCK, SLOTS * BLOCK), 1)
-        return lanes < pat_s[k, r, SLOTS] * BLOCK
+        return lanes < pat_s[k, SLOTS, r] * BLOCK
 
     def each_row(body):
         def several(i, carry):
@@ -296,16 +301,7 @@
             ref, row = share(u, 0, kept)
             cols = pl.ds(pl.multiple_of(kept * HALF, 128), HALF)
             add_rows(ref, row, cols, [(rb3.at[u], 0, A)], 64)
-            i = count["remote"]
-            count["remote"] += 1
-            cp = pltpu.make_async_remote_copy(
-                src_ref=share_at(u, 0, kept), dst_ref=gi_ref.at[pl.ds(row, 64)],
-                send_sem=send.at[i], recv_sem=local.at[0],
-                device_id=dev(x, 1 - zh, zl, (y + 4 + odd * (2 * kept - 1)) % 4, kept),
-                device_id_type=MESH,
-            )
-            cp.start()
-            sends.append(cp)
+            remote(("hop", u), share_at(u, 0, kept), rb4.at[u - 4], zhp)
             return
         cp3, stays = crossing[u]
 
@@ -337,6 +333,29 @@
                 cp.start()
 
             finals.append((cp, away))
+
+    def deliver(u):
+        need(("hop", u))
+        away_y = (1 - odd) * (1 - 2 * kept)
+        src, dst = rb4.at[u - 4], gi_ref.at[rows_of(c * 256 + (u - 4) * 64, 64)]
+        i = count["remote"]
+        count["remote"] += 1
+        cp = pltpu.make_async_remote_copy(
+            src_ref=src, dst_ref=dst, send_sem=send.at[i], recv_sem=local.at[0],
+            device_id=dev(x, zh, zl, (y + 4 + away_y) % 4, 1 - kept), device_id_type=MESH,
+        )
+        stay = pltpu.make_async_copy(src, dst, local.at[0])
+        moves = jnp.logical_not(stay_put)
+
+        @pl.when(stay_put)
+        def _():
+            stay.start()
+
+        @pl.when(moves)
+        def _():
+            cp.start()
+
+        finals.append((cp, moves))
 
     def spread(k):
         need(("t0", k))
@@ -499,18 +518,22 @@
     step_right(6)
     step_left(6)
     end_ring(5)
+    to_owner(4)
     step_right(7)
     step_left(7)
-    end_ring(6)
-    to_owner(4)
-    to_owner(5)
-    end_ring(7)
     to_owner(0)
     to_owner(1)
+    end_ring(6)
+    to_owner(5)
+    deliver(4)
     to_owner(2)
     to_owner(3)
+    end_ring(7)
     to_owner(6)
+    deliver(5)
     to_owner(7)
+    deliver(6)
+    deliver(7)
     need("dl", "d2r")
     finish(0, 3, 4)
     need("dr", "d2l")
@@ -528,13 +551,11 @@
             cp.wait_send()
 
 
-N_REMOTE = 136
+N_REMOTE = 144
 N_LOCAL = 24
 
 
 def per_device(tokens, preact, grad_hidden, w_packed, block_cols, block_counts):
-    pattern = jnp.concatenate([block_cols, block_counts], axis=1)
-    pattern = jnp.pad(pattern, ((0, 16 - ROWS_DEV), (0, BLOCK - SLOTS - 1)))
     any_space = pl.BlockSpec(memory_space=pl.ANY)
     vmem = pl.BlockSpec(memory_space=pltpu.VMEM)
     bf16 = jnp.bfloat16
@@ -545,11 +566,12 @@
             jax.ShapeDtypeStruct((WIDE, SLOTS * BLOCK), bf16),
             jax.ShapeDtypeStruct((4, PANEL, WIDE), bf16),
         ),
-        in_specs=[vmem] + [any_space] * 4,
+        in_specs=[vmem] * 2 + [any_space] * 4,
         out_specs=(any_space, vmem, any_space),
         scratch_shapes=[
-            pltpu.VMEM((3, 16, BLOCK), jnp.int32),
-            pltpu.SMEM((4, 16, BLOCK), jnp.int32),
+            pltpu.VMEM((8, BLOCK), jnp.int32),
+            pltpu.VMEM((3, 8, BLOCK), jnp.int32),
+            pltpu.SMEM((4, 8, BLOCK), jnp.int32),
             pltpu.VMEM((4, WIDE, SLOTS * BLOCK), bf16),
             pltpu.VMEM((COLS, PANEL, BLOCK), bf16),
             pltpu.VMEM((COLS, PANEL, BLOCK), bf16),
@@ -558,6 +580,7 @@
             pltpu.VMEM((8, 256, WIDE), bf16),
             pltpu.VMEM((8, 6, 64, HALF), bf16),
             pltpu.VMEM((8, 64, WIDE), bf16),
+            pltpu.VMEM((4, 64, HALF), bf16),
             pltpu.VMEM((4, WIDE, SLOTS * BLOCK), bf16),
             pltpu.VMEM((6, HALF, SLOTS * BLOCK), bf16),
             pltpu.SemaphoreType.DMA((N_REMOTE,)),
@@ -568,7 +591,7 @@
             collective_id=0, has_side_effects=True, vmem_limit_bytes=60 << 20
         ),
         name="ffn_backward",
-    )(pattern, tokens, preact, grad_hidden, w_packed)
+    )(block_cols.T, block_counts.T, tokens, preact, grad_hidden, w_packed)
     return grad_input, grad_weight
 
 

time: 135 us -> 128 us (0.948)
  Pallas kernels: 128 us -> 122 us
  local copies, waits for them, and re-layouts: 5.45 us -> 3.33 us
    pallas_call x1, Pallas kernels: 128 us -> 122 us  [per_device(): pl.pallas_call(kernel, out_shape=(jax.ShapeDtypeStruct((PANEL, HALF), bf1...]
    unnamed x6 -> x4, local copies, waits for them, and re-layouts: 4.84 us -> 3.33 us
where the time goes in v4:
time: 128 us; the launch traced here: 126 us
  Pallas kernels  122 us (95%)
  local copies, waits for them, and re-layouts  3.33 us (3%)
    pallas_call x1, Pallas kernels, per_device(): pl.pallas_call(kernel, out_shape=(jax.ShapeDtypeStruct((PANEL, HALF), bf1...  122 us
    unnamed x4, local copies, waits for them, and re-layouts  3.33 us

profile of v4, /device:TPU:2, one launch (start us, length us, event | category | flops | bytes accessed | tf_op | source)
XLA Modules:
  0.0 126.3 jit_solution(3006677420986220133)
XLA Ops:
  0.6 122.3 %ffn_backward.1 = (bf16[512,768]{1,0:T(8,128)(2,1)}, bf16[1536,512]{1,0:T(8,128)(2,1)}, bf16[4,512,1536]{2,1,0:T(8,128)(2,1)}) custom-call(s32[4,12]{1,0:T(4,128)} %bitcast.2, s32[1,12]{1,0:T(1,128)} %bitcast.3, bf16[512,12288]{1,0:T(8,128)(2,1)} %tokens.1, bf16[512,1536]{1,0:T(8,128)(2,1)} %preact.1, bf16[512,1536]{1,0:T(8,128)(2,1)} %grad_hidden.1, ...), custom_call_target="tpu_custom_call" | custom-call | tf_op jit(solution)/shard_map/ffn_backward/pallas_call | solution.py:562
  123.0 0.0 copy-start
  123.0 2.2 %copy.10 = bf16[512,768]{1,0:T(8,128)(2,1)} copy(bf16[512,768]{1,0:T(8,128)(2,1)} %get-tuple-element.8) | data formatting | bytes 1572864
  125.2 0.0 copy-done
  125.2 1.1 copy.11
Async XLA Ops:
  123.0 2.2 %copy-start = (bf16[1536,512]{1,0:T(8,128)(2,1)S(1)}, bf16[1536,512]{1,0:T(8,128)(2,1)}, u32[]{:S(2)}) copy-start(bf16[1536,512]{1,0:T(8,128)(2,1)} %get-tuple-element.9) | copy-start | bytes 4718596

commit v5 on v4

--- a/solution.py
+++ b/solution.py
@@ -429,10 +429,11 @@
             there = pl.ds(pl.multiple_of(i * 32, 32), 32)
             total = dw[OWN, here, :].astype(jnp.float32) + dx[first_, there, :].astype(jnp.float32)
             total = total + dx[second_, there, :].astype(jnp.float32)
-            gw_ref[here, :] = total.astype(jnp.bfloat16)
+            dw[OWN, here, :] = total.astype(jnp.bfloat16)
             return carry
 
         lax.fori_loop(0, HALF // 32, body, 0)
+        near(("gw", row), dw.at[OWN, pl.ds(row, HALF)], gw_ref.at[pl.ds(row, HALF)])
 
     start_patterns()
     start_weights()
@@ -567,7 +568,7 @@
             jax.ShapeDtypeStruct((4, PANEL, WIDE), bf16),
         ),
         in_specs=[vmem] * 2 + [any_space] * 4,
-        out_specs=(any_space, vmem, any_space),
+        out_specs=(any_space,) * 3,
         scratch_shapes=[
             pltpu.VMEM((8, BLOCK), jnp.int32),
             pltpu.VMEM((3, 8, BLOCK), jnp.int32),

time: 128 us -> 126 us (0.984)
  no operation moved by 1% of the time
where the time goes in v5:
time: 126 us; the launch traced here: 125 us
  Pallas kernels  121 us (96%)
  local copies, waits for them, and re-layouts  3.33 us (3%)
    pallas_call x1, Pallas kernels, per_device(): pl.pallas_call(kernel, out_shape=(jax.ShapeDtypeStruct((PANEL, HALF), bf1...  121 us
    unnamed x4, local copies, waits for them, and re-layouts  3.33 us

profile of v5, /device:TPU:2, one launch (start us, length us, event | category | flops | bytes accessed | tf_op | source)
XLA Modules:
  0.0 125.2 jit_solution(10351947278199105543)
XLA Ops:
  0.6 121.2 %ffn_backward.1 = (bf16[512,768]{1,0:T(8,128)(2,1)}, bf16[1536,512]{1,0:T(8,128)(2,1)}, bf16[4,512,1536]{2,1,0:T(8,128)(2,1)}) custom-call(s32[4,12]{1,0:T(4,128)} %bitcast.2, s32[1,12]{1,0:T(1,128)} %bitcast.3, bf16[512,12288]{1,0:T(8,128)(2,1)} %tokens.1, bf16[512,1536]{1,0:T(8,128)(2,1)} %preact.1, bf16[512,1536]{1,0:T(8,128)(2,1)} %grad_hidden.1, ...), custom_call_target="tpu_custom_call" | custom-call | tf_op jit(solution)/shard_map/ffn_backward/pallas_call | solution.py:563
  121.8 0.0 copy-start
  121.8 2.2 %copy.10 = bf16[512,768]{1,0:T(8,128)(2,1)} copy(bf16[512,768]{1,0:T(8,128)(2,1)} %get-tuple-element.8) | data formatting | bytes 1572864
  124.0 0.0 copy-done
  124.0 1.1 copy.11
Async XLA Ops:
  121.8 2.2 %copy-start = (bf16[1536,512]{1,0:T(8,128)(2,1)S(1)}, bf16[1536,512]{1,0:T(8,128)(2,1)}, u32[]{:S(2)}) copy-start(bf16[1536,512]{1,0:T(8,128)(2,1)} %get-tuple-element.9) | copy-start | bytes 4718596
